TPU v7x, 32 devices: a whole 2x2x4 slice. The times are simulated.
32 devices in a mesh: parts: 2 (over y), space: 8 (over z, x), tm: 2 (over core).
Axes of the slice: x: 2, y: 2, z: 4, core: 2. Of those that a mesh axis runs over, the one named last changes fastest.
Arguments:
- eigvecs: bfloat16 [4, 2, 256, 3, 1728], P(('parts', 'tm'), None, None, None, 'space'), parts along dimension 0, may hold values from -1.25 to 1.25
- links: bfloat16 [4, 3, 3, 3, 2, 1728], P(('parts', 'tm'), None, None, None, None, 'space'), parts along dimension 0, may hold values from -2.5 to 2.5
- dirs: int32 [3], replicated, may hold values from 0 to 2, each once
- peram: bfloat16 [4, 2, 1024, 1024], P(('parts', 'tm'), None, 'space'), parts along dimension 0, may hold values from -0.25 to 0.25
Outputs:
- meson_blocks: bfloat16 [4, 3, 2, 1024, 1024], P(('parts', 'tm'), None, None, 'space'), parts along dimension 0
There are 2 independent parts, one for each index of `parts`. A program takes and returns all parts, laid end to end along the dimension named above; an argument that names none is the same for every part. Nothing has to cross between parts.
All inputs are finite; a program needn't handle non-finite values.
Results may differ from a plain program's by a relative error of at most 0.0061.
Values may be sent and summed in bfloat16 or wider, within the bound.
A program may use at most 64 MiB of HBM per device.

v0:
```python
import jax
import jax.numpy as jnp
from jax import lax
from jax.sharding import PartitionSpec as P

K = 256
SPIN = 4
LX = 9
LZ = 24


def from_behind(block, axis, distance):
    devices = range(lax.axis_size(axis))
    route = [((i - distance) % len(devices), i) for i in devices]
    return lax.ppermute(block, axis, route)


def link_apply(link_mat, values_in, adjoint):
    real_rows = []
    imag_rows = []
    for out_row in range(3):
        real_sum = jnp.zeros(values_in.shape[1:2] + values_in.shape[3:], jnp.float32)
        imag_sum = jnp.zeros(values_in.shape[1:2] + values_in.shape[3:], jnp.float32)
        for in_col in range(3):
            if adjoint:
                link_entry = link_mat[in_col, out_row]
                conj_sign = -1.0
            else:
                link_entry = link_mat[out_row, in_col]
                conj_sign = 1.0
            link_real = link_entry[0].astype(jnp.float32)[None]
            link_imag = (conj_sign * link_entry[1].astype(jnp.float32))[None]
            vec_real = values_in[0, :, in_col].astype(jnp.float32)
            vec_imag = values_in[1, :, in_col].astype(jnp.float32)
            real_sum = real_sum + link_real * vec_real - link_imag * vec_imag
            imag_sum = imag_sum + link_real * vec_imag + link_imag * vec_real
        real_rows.append(real_sum)
        imag_rows.append(imag_sum)
    return jnp.stack([jnp.stack(real_rows, axis=1), jnp.stack(imag_rows, axis=1)])


def contract(left, right):
    return lax.dot_general(
        left, right, (((1,), (1,)), ((), ())), preferred_element_type=jnp.float32
    )


def elemental(eigen_field, derivative):
    vectors = eigen_field.shape[1]
    vec_real = eigen_field[0].reshape(vectors, -1)
    vec_imag = eigen_field[1].reshape(vectors, -1)
    der_real = derivative[0].reshape(vectors, -1)
    der_imag = derivative[1].reshape(vectors, -1)
    return jnp.stack(
        [
            contract(vec_real, der_real) + contract(vec_imag, der_imag),
            contract(vec_real, der_imag) - contract(vec_imag, der_real),
        ]
    )


def lattice(values):
    return values.reshape(values.shape[:-1] + (values.shape[-1] // (LX * LZ), LX, LZ))


def on_device(eigvecs, links, dirs, peram):
    eig_lat = lattice(eigvecs)
    link_lat = lattice(links)
    slab_rows = eig_lat.shape[4]
    back_y = jnp.stack([link_apply(link_lat[0, 1], eig_lat[0], True).astype(jnp.bfloat16)])
    y_ahead = from_behind(eig_lat[:, :, :, :, 0], "space", -1)
    y_behind = from_behind(back_y[:, :, :, :, slab_rows - 1], "space", 1)
    choose = dirs[:, None] == jnp.arange(3, dtype=jnp.int32)[None, :]
    position = 0
    eigen_field = eig_lat[position]
    link_set = link_lat[position]
    elementals = []
    for direction in range(3):
        if direction == 0:
            ahead_field = jnp.roll(eigen_field, -1, axis=4)
            back_term = link_apply(link_set[0], eigen_field, True).astype(jnp.bfloat16)
            behind = jnp.roll(back_term, 1, axis=4)
        elif direction == 1:
            ahead_field = jnp.concatenate(
                [eigen_field[:, :, :, 1:], y_ahead[position][:, :, :, None]], axis=3
            )
            behind = jnp.concatenate(
                [y_behind[position][:, :, :, None], back_y[position][:, :, :, :-1]], axis=3
            )
        else:
            ahead_field = jnp.roll(eigen_field, -1, axis=5)
            back_term = link_apply(link_set[2], eigen_field, True).astype(jnp.bfloat16)
            behind = jnp.roll(back_term, 1, axis=5)
        derivative = (
            link_apply(link_set[direction], ahead_field, False) - behind.astype(jnp.float32)
        ).astype(jnp.bfloat16)
        elementals.append(elemental(eigen_field, derivative))
    elementals = jnp.stack(elementals)
    picked_all = [jnp.sum(jnp.where(choose[:, :, None, None, None], elementals[None], 0.0), axis=1)]
    stacked = jnp.stack(picked_all)
    elem_low = lax.psum(stacked, "space").astype(jnp.bfloat16)
    blocks = from_behind(peram, "tm", -1)
    columns = blocks.shape[2]
    position = 0
    elem_real = elem_low[position, :, 0]
    elem_imag = elem_low[position, :, 1]
    peram_real = blocks[position, 0].reshape(columns, K, SPIN)
    peram_imag = blocks[position, 1].reshape(columns, K, SPIN)
    out_real = jnp.einsum(
        "jkl,cls->jcks", elem_real, peram_real, preferred_element_type=jnp.float32
    ) - jnp.einsum("jkl,cls->jcks", elem_imag, peram_imag, preferred_element_type=jnp.float32)
    out_imag = jnp.einsum(
        "jkl,cls->jcks", elem_real, peram_imag, preferred_element_type=jnp.float32
    ) + jnp.einsum("jkl,cls->jcks", elem_imag, peram_real, preferred_element_type=jnp.float32)
    combined = jnp.stack([out_real, out_imag], axis=1)
    results = [combined.reshape(combined.shape[0], 2, columns, K * SPIN).astype(jnp.bfloat16)]
    return jnp.stack(results)


def solution(mesh):
    placed = (
        P(("parts", "tm"), None, None, None, "space"),
        P(("parts", "tm"), None, None, None, None, "space"),
        P(),
        P(("parts", "tm"), None, "space", None),
    )
    return jax.shard_map(
        on_device,
        mesh=mesh,
        in_specs=placed,
        out_specs=P(("parts", "tm"), None, None, "space", None),
        check_vma=False,
    )
```

profile of v0, /device:TPU:0, one launch (start us, length us, event | category | flops | bytes accessed | tf_op | source)
XLA Modules:
  0.0 128.9 jit_solution(4704577270389625453)
XLA Ops:
  0.0 1.0 reshape.4464
  1.1 1.5 %fusion.160 = (bf16[256,1,1,9,24]{0,4,3,1,2:T(8,128)(2,1)S(1)}, bf16[256,1,1,9,24]{0,4,3,1,2:T(8,128)(2,1)S(1)}) fusion(f32[9,24]{1,0:T(8,128)S(1)} %get-tuple-element.98, f32[9,24]{1,0:T(8,128)S(1)} %get-tuple-element.89, f32[9,24]{1,0:T(8,128)S(1)} %get-tuple-element.99, f32[9,24]{1,0:T(8,128)S(1)} %get-tuple-element.90, ...), kind=kLoop, calls=%fused_computation.422 | loop fusion | flops 1658880 | bytes 889920 | tf_op jit(solution)/shard_map/convert.111
  3.3 0.9 pad_maximum_fusion.7
  4.2 2.9 %collective-permute-start.1 = (bf16[1,2,256,3,9,24]{2,5,4,3,1,0:T(8,128)(2,1)}, bf16[1,2,256,3,9,24]{2,5,4,3,1,0:T(8,128)(2,1)}, u32[]{:S(2)}, u32[]{:S(2)}) collective-permute-start(bf16[1,2,256,3,9,24]{2,5,4,3,1,0:T(8,128)(2,1)} %pad_maximum_fusion.7), channel_id=1, source_target_pairs={{14,0},{0,2},{2,4},{4,6},{6,8},{8,10},{10,12},{12,14},{15,1},{1,3}... | collective-permute-start | bytes 1990664 | tf_op jit(solution)/shard_map/ppermute | solution.py:15
  7.2 3.0 %collective-permute-start = (bf16[1,2,256,3,9,24]{2,5,4,3,1,0:T(8,128)(2,1)S(1)}, bf16[1,2,256,3,9,24]{2,5,4,3,1,0:T(8,128)(2,1)S(1)}, u32[]{:S(2)}, u32[]{:S(2)}) collective-permute-start(bf16[1,2,256,3,9,24]{2,5,4,3,1,0:T(8,128)(2,1)S(1)} %bitcast.1013), channel_id=1, source_target_pairs={{2,0},{4,2},{6,4},{8,6},{10,8},{12,10},{14,12},{0,14},{3,1},{5,3},... | collective-permute-start | bytes 1990664 | tf_op jit(solution)/shard_map/ppermute | solution.py:15
  10.2 1.0 copy.140
  11.2 0.6 fusion.315
  12.0 0.6 fusion.296
  12.7 0.6 fusion.295
  13.3 0.6 broadcast_multiply_fusion.17
  13.9 0.6 broadcast_multiply_fusion.9
  14.7 0.6 broadcast_multiply_fusion.8
  15.4 0.6 fusion.250
  16.5 0.9 fusion.25
  17.5 0.9 fusion.30
  18.4 0.9 fusion.27
  19.4 0.9 fusion.35
  22.0 0.4 fusion.45
  28.1 0.8 maximum_bitcast_fusion.6
  28.9 0.8 maximum_bitcast_fusion.8
  29.9 1.1 fusion.314
  31.1 0.9 copy.141
  32.0 5.7 %collective-permute-done = bf16[1,2,256,3,9,24]{2,5,4,3,1,0:T(8,128)(2,1)S(1)} collective-permute-done((bf16[1,2,256,3,9,24]{2,5,4,3,1,0:T(8,128)(2,1)S(1)}, bf16[1,2,256,3,9,24]{2,5,4,3,1,0:T(8,128)(2,1)S(1)}, u32[]{:S(2)}, u32[]{:S(2)}) %collective-permute-start) | collective-permute-done | bytes 663584 | tf_op jit(solution)/shard_map/ppermute | solution.py:15
  38.8 1.3 %fusion.1 = bf16[2,256,3,1,9,24]{1,5,4,2,0,3:T(8,128)(2,1)S(1)} fusion(f32[1,256,3,1,9,24]{1,5,4,2,0,3:T(8,128)S(1)} %get-tuple-element.151, f32[1,256,3,1,9,24]{1,5,4,2,0,3:T(8,128)S(1)} %get-tuple-element.150, bf16[1,2,256,3,9,24]{2,5,4,3,1,0:T(8,128)(2,1)} %collective-permute-done.1), kind=kLoop, calls=%fused_computation.14 | loop fusion | flops 1327104 | bytes 2654208 | tf_op jit(solution)/shard_map/convert_element_type | solution.py:96
  42.1 0.5 copy.138
  42.6 0.4 select_reduce_fusion
  43.4 80.4 %all-reduce.1 = bf16[1,3,2,256,256]{4,3,1,2,0:T(8,128)(2,1)S(1)} all-reduce(f32[1,3,2,256,256]{4,3,1,2,0:T(8,128)S(1)} %bitcast.1036), channel_id=1, replica_groups=mesh['parts'=2,'space'=8,'tm'=2] {'space'}, use_global_device_ids=true, to_apply=%region_1.2 | all-reduce | flops 393216 | bytes 2359296 | tf_op jit(solution)/shard_map/psum | solution.py:101
  124.2 0.5 copy-done.1
  125.1 0.4 fusion.3
  125.5 0.6 copy.143
  126.5 0.6 copy.146
  127.3 1.6 %copy.147 = bf16[1,3,2,128,1024]{4,3,2,1,0:T(8,128)(2,1)} copy(bf16[1,3,2,128,1024]{3,4,1,2,0:T(8,128)(2,1)S(1)} %pad_maximum_fusion.1) | data formatting | bytes 3145728 | tf_op jit(solution)/shard_map/stack | solution.py:115
  (153 shorter events, 13.2 us)
Async XLA Ops:
  0.0 2.6 %copy-start = (bf16[1,2,256,3,216]{2,4,3,1,0:T(8,128)(2,1)S(1)}, bf16[1,2,256,3,216]{2,4,3,1,0:T(8,128)(2,1)}, u32[]{:S(2)}) copy-start(bf16[1,2,256,3,216]{2,4,3,1,0:T(8,128)(2,1)} %param.4) | copy-start | bytes 1990660
  2.9 7.3 %copy-start.8 = (bf16[1,2,128,1024]{3,2,1,0:T(8,128)(2,1)S(1)}, bf16[1,2,128,1024]{3,2,1,0:T(8,128)(2,1)}, u32[]{:S(2)}) copy-start(bf16[1,2,128,1024]{3,2,1,0:T(8,128)(2,1)} %param.7) | copy-start | bytes 1572868
  3.2 8.0 %copy-start.9 = (bf16[1,3,3,3,2,216]{5,4,3,2,1,0:T(2,128)(2,1)S(1)}, bf16[1,3,3,3,2,216]{5,4,3,2,1,0:T(2,128)(2,1)}, u32[]{:S(2)}) copy-start(bf16[1,3,3,3,2,216]{5,4,3,2,1,0:T(2,128)(2,1)} %param.5) | copy-start | bytes 69988
  4.2 34.6 %collective-permute-start.1 = (bf16[1,2,256,3,9,24]{2,5,4,3,1,0:T(8,128)(2,1)}, bf16[1,2,256,3,9,24]{2,5,4,3,1,0:T(8,128)(2,1)}, u32[]{:S(2)}, u32[]{:S(2)}) collective-permute-start(bf16[1,2,256,3,9,24]{2,5,4,3,1,0:T(8,128)(2,1)} %pad_maximum_fusion.7), channel_id=1, source_target_pairs={{14,0},{0,2},{2,4},{4,6},{6,8},{8,10},{10,12},{12,14},{15,1},{1,3}... | collective-permute-start | bytes 1990664 | tf_op jit(solution)/shard_map/ppermute | solution.py:15
  7.2 30.6 %collective-permute-start = (bf16[1,2,256,3,9,24]{2,5,4,3,1,0:T(8,128)(2,1)S(1)}, bf16[1,2,256,3,9,24]{2,5,4,3,1,0:T(8,128)(2,1)S(1)}, u32[]{:S(2)}, u32[]{:S(2)}) collective-permute-start(bf16[1,2,256,3,9,24]{2,5,4,3,1,0:T(8,128)(2,1)S(1)} %bitcast.1013), channel_id=1, source_target_pairs={{2,0},{4,2},{6,4},{8,6},{10,8},{12,10},{14,12},{0,14},{3,1},{5,3},... | collective-permute-start | bytes 1990664 | tf_op jit(solution)/shard_map/ppermute | solution.py:15
  11.2 18.7 %collective-permute-start.2 = (bf16[1,2,128,1024]{2,3,1,0:T(8,128)(2,1)}, bf16[1,2,128,1024]{2,3,1,0:T(8,128)(2,1)}, u32[]{:S(2)}, u32[]{:S(2)}) collective-permute-start(bf16[1,2,128,1024]{2,3,1,0:T(8,128)(2,1)} %copy.140), channel_id=1, source_target_pairs={{1,0},{0,1},{3,2},{2,3},{5,4},{4,5},{7,6},{6,7},{9,8},{8,9},{11,10... | collective-permute-start | bytes 1572872 | tf_op jit(solution)/shard_map/ppermute | solution.py:15
  17.4 2.8 %copy-start.10 = (f32[9,24]{1,0:T(8,128)S(1)}, f32[9,24]{1,0:T(8,128)}, u32[]{:S(2)}) copy-start(f32[9,24]{1,0:T(8,128)} %get-tuple-element.64) | copy-start | bytes 2596
  17.4 2.8 %copy-start.14 = (f32[9,24]{1,0:T(8,128)S(1)}, f32[9,24]{1,0:T(8,128)}, u32[]{:S(2)}) copy-start(f32[9,24]{1,0:T(8,128)} %get-tuple-element.68) | copy-start | bytes 2596
  17.4 2.8 %copy-start.39 = (f32[9,24]{1,0:T(8,128)S(1)}, f32[9,24]{1,0:T(8,128)}, u32[]{:S(2)}) copy-start(f32[9,24]{1,0:T(8,128)} %get-tuple-element.56) | copy-start | bytes 2596
  17.5 2.8 %copy-start.40 = (f32[9,24]{1,0:T(8,128)S(1)}, f32[9,24]{1,0:T(8,128)}, u32[]{:S(2)}) copy-start(f32[9,24]{1,0:T(8,128)} %get-tuple-element.58) | copy-start | bytes 2596
  17.5 2.8 %copy-start.41 = (f32[9,24]{1,0:T(8,128)S(1)}, f32[9,24]{1,0:T(8,128)}, u32[]{:S(2)}) copy-start(f32[9,24]{1,0:T(8,128)} %get-tuple-element.61) | copy-start | bytes 2596
  18.4 2.3 %copy-start.12 = (f32[9,24]{1,0:T(8,128)S(1)}, f32[9,24]{1,0:T(8,128)}, u32[]{:S(2)}) copy-start(f32[9,24]{1,0:T(8,128)} %get-tuple-element.66) | copy-start | bytes 2596
  18.4 2.3 %copy-start.13 = (f32[9,24]{1,0:T(8,128)S(1)}, f32[9,24]{1,0:T(8,128)}, u32[]{:S(2)}) copy-start(f32[9,24]{1,0:T(8,128)} %get-tuple-element.67) | copy-start | bytes 2596
  18.4 2.3 %copy-start.36 = (f32[9,24]{1,0:T(8,128)S(1)}, f32[9,24]{1,0:T(8,128)}, u32[]{:S(2)}) copy-start(f32[9,24]{1,0:T(8,128)} %get-tuple-element.57) | copy-start | bytes 2596
  18.4 2.3 %copy-start.37 = (f32[9,24]{1,0:T(8,128)S(1)}, f32[9,24]{1,0:T(8,128)}, u32[]{:S(2)}) copy-start(f32[9,24]{1,0:T(8,128)} %get-tuple-element.60) | copy-start | bytes 2596
  18.4 2.3 %copy-start.38 = (f32[9,24]{1,0:T(8,128)S(1)}, f32[9,24]{1,0:T(8,128)}, u32[]{:S(2)}) copy-start(f32[9,24]{1,0:T(8,128)} %get-tuple-element.63) | copy-start | bytes 2596
  23.2 1.2 copy-start.26
  23.3 1.2 copy-start.27
  23.3 1.2 copy-start.28
  23.6 1.2 copy-start.23
  23.6 1.2 copy-start.24
  23.6 1.2 copy-start.25
  23.9 1.2 copy-start.17
  23.9 1.2 copy-start.18
  23.9 1.2 copy-start.19
  24.3 1.2 copy-start.20
  24.3 1.2 copy-start.21
  24.3 1.2 copy-start.22
  24.8 1.1 copy-start.6
  25.2 1.1 copy-start.5
  27.8 2.0 %copy-start.44 = (s32[3]{0:T(128)S(1)}, s32[3]{0:T(128)}, u32[]{:S(2)}) copy-start(s32[3]{0:T(128)} %param.6) | copy-start | bytes 40
  40.8 1.2 copy-start.3
  (16 other events, 15.9 us)
where the time goes:
time: 129 us
  blocking collectives  80.4 us (62%)
  other arithmetic  19.6 us (15%)
  local copies, waits for them, and re-layouts  10.9 us (8%)
  starting transfers between devices  5.98 us (5%)
  waiting for transfers between devices  5.74 us (4%)
  matrix products  5.25 us (4%)
    psum x1, blocking collectives, on_device(): elem_low = lax.psum(stacked, 'space').astype(jnp.bfloat16)  80.4 us
    ppermute x3, starting transfers between devices, from_behind(): return lax.ppermute(block, axis, route)  5.98 us
    ppermute x3, waiting for transfers between devices, from_behind(): return lax.ppermute(block, axis, route)  5.74 us
    another operation x9, other arithmetic  3.94 us
    sub x8, other arithmetic, link_apply(): real_sum = real_sum + link_real * vec_real - link_imag * vec_imag  3.79 us
    dot_general x12, matrix products, contract(): lax.dot_general(left, right, (((1,), (1,)), ((), ())), preferred_element_...  3.66 us
    unnamed x91, local copies, waits for them, and re-layouts  2.59 us
  transfers between devices with their start and end apart: 3, of which 1 were waited for; matrix products, arithmetic and copies ran while one was open for 17% of the time, Pallas kernels for 0%

commit v1 on v0

--- a/solution.py
+++ b/solution.py
@@ -1,12 +1,18 @@
+import functools
+
 import jax
 import jax.numpy as jnp
+import numpy as np
 from jax import lax
+from jax.experimental import pallas as pl
+from jax.experimental.pallas import tpu as pltpu
 from jax.sharding import PartitionSpec as P
 
 K = 256
 SPIN = 4
 LX = 9
 LZ = 24
+MESH = pl.DeviceIdType.MESH
 
 
 def from_behind(block, axis, distance):
@@ -63,7 +69,7 @@
     return values.reshape(values.shape[:-1] + (values.shape[-1] // (LX * LZ), LX, LZ))
 
 
-def on_device(eigvecs, links, dirs, peram):
+def general(eigvecs, links, dirs, peram):
     eig_lat = lattice(eigvecs)
     link_lat = lattice(links)
     slab_rows = eig_lat.shape[4]
@@ -99,7 +105,10 @@
     picked_all = [jnp.sum(jnp.where(choose[:, :, None, None, None], elementals[None], 0.0), axis=1)]
     stacked = jnp.stack(picked_all)
     elem_low = lax.psum(stacked, "space").astype(jnp.bfloat16)
-    blocks = from_behind(peram, "tm", -1)
+    return finish(elem_low, from_behind(peram, "tm", -1))
+
+
+def finish(elem_low, blocks):
     columns = blocks.shape[2]
     position = 0
     elem_real = elem_low[position, :, 0]
@@ -117,6 +126,247 @@
     return jnp.stack(results)
 
 
+def halo_plan(eigvecs):
+    n = lax.axis_size("space")
+    return (
+        eigvecs.shape[-1] == LX * LZ
+        and lax.axis_size("tm") == 2
+        and n > 1
+        and eigvecs.shape[0] == 1
+        and K % (16 * n) == 0
+    )
+
+
+def mix(link_ref, direction, adjoint, lanes, source, target):
+    lo, hi = lanes
+
+    @pl.loop(0, K // 16)
+    def _(step):
+        rows = pl.ds(pl.multiple_of(step * 16, 16), 16)
+        vec = [[source(ri, c, rows).astype(jnp.float32) for c in range(3)] for ri in range(2)]
+        for out_row in range(3):
+            real_sum = None
+            for in_col in range(3):
+                a, b = (in_col, out_row) if adjoint else (out_row, in_col)
+                at = ((direction * 3 + a) * 3 + b) * 2
+                link_real = link_ref[at : at + 1, lo:hi]
+                link_imag = link_ref[at + 1 : at + 2, lo:hi]
+                rr = link_real * vec[0][in_col]
+                ii = link_imag * vec[1][in_col]
+                ri = link_real * vec[1][in_col]
+                ir = link_imag * vec[0][in_col]
+                real = rr + ii if adjoint else rr - ii
+                imag = ri - ir if adjoint else ri + ir
+                real_sum = real if real_sum is None else real_sum + real
+                imag_sum = imag if in_col == 0 else imag_sum + imag
+            target[0, out_row, rows, :] = real_sum.astype(jnp.bfloat16)
+            target[1, out_row, rows, :] = imag_sum.astype(jnp.bfloat16)
+
+
+def overlap(left, right):
+    real = imag = None
+    for c in range(3):
+        lr, li, rr, ri = left(0, c), left(1, c), right(0, c), right(1, c)
+        re = contract(lr, rr) + contract(li, ri)
+        im = contract(lr, ri) - contract(li, rr)
+        real = re if real is None else real + re
+        imag = im if imag is None else imag + im
+    return real, imag
+
+
+def halo_kernel(
+    n, v_ref, link_ref, perm_ref, peram_ref, elem_ref, swapped_ref,
+    shifted, mixed, mixed_lo, up_out, up_in, down_in, part, gathered, low, landed,
+    halo_send, halo_recv, rs_send, rs_recv, ag_send, ag_recv,
+):
+    me = lax.axis_index("space")
+    core = lax.axis_index("tm")
+    chunk = K // n
+    split = 128
+    sites = LX * LZ
+
+    barrier = pltpu.get_barrier_semaphore()
+    for o in range(1, n):
+        pl.semaphore_signal(
+            barrier, inc=1, device_id={"space": lax.rem(me + o, n)}, device_id_type=MESH
+        )
+    pl.semaphore_signal(barrier, inc=1, device_id={"tm": 1 - core}, device_id_type=MESH)
+    pl.semaphore_wait(barrier, n)
+
+    down = pltpu.make_async_remote_copy(
+        src_ref=v_ref.at[:, :, :, pl.ds(0, split)],
+        dst_ref=down_in,
+        send_sem=halo_send.at[0],
+        recv_sem=halo_recv.at[0],
+        device_id={"space": lax.rem(me + n - 1, n)},
+        device_id_type=MESH,
+    )
+    down.start()
+    mix(link_ref, 1, True, (split, sites), lambda ri, c, rows: v_ref[ri, c, rows, split:sites], up_out)
+    up = pltpu.make_async_remote_copy(
+        src_ref=up_out,
+        dst_ref=up_in,
+        send_sem=halo_send.at[1],
+        recv_sem=halo_recv.at[1],
+        device_id={"space": lax.rem(me + 1, n)},
+        device_id_type=MESH,
+    )
+    up.start()
+    swap = pltpu.make_async_remote_copy(
+        src_ref=peram_ref,
+        dst_ref=swapped_ref,
+        send_sem=halo_send.at[2],
+        recv_sem=halo_recv.at[2],
+        device_id={"tm": 1 - core},
+        device_id_type=MESH,
+    )
+    swap.start()
+
+    row = lax.broadcasted_iota(jnp.int32, (K, K), 0)
+    col = lax.broadcasted_iota(jnp.int32, (K, K), 1)
+
+    def scatter(direction, real, imag):
+        turned = jnp.where(row > col, -real, imag).T
+        part[direction] = (jnp.where(row < col, real, imag) + turned).astype(jnp.bfloat16)
+        copies = []
+        for o in range(1, n):
+            peer = lax.rem(me + o, n)
+            copy = pltpu.make_async_remote_copy(
+                src_ref=part.at[direction, pl.ds(pl.multiple_of(peer * chunk, chunk), chunk)],
+                dst_ref=landed.at[direction, o],
+                send_sem=rs_send.at[direction, o],
+                recv_sem=rs_recv.at[direction, o],
+                device_id={"space": peer},
+                device_id_type=MESH,
+            )
+            copy.start()
+            copies.append(copy)
+        return copies
+
+    def gather(direction, copies):
+        mine = pl.ds(pl.multiple_of(me * chunk, chunk), chunk)
+        total = part[direction, mine].astype(jnp.float32)
+        for o in range(1, n):
+            copies[o - 1].wait_recv()
+            total = total + landed[direction, o].astype(jnp.float32)
+        low[direction] = total.astype(jnp.bfloat16)
+        gathered[direction, mine] = low[direction]
+        sends = []
+        for o in range(1, n):
+            copy = pltpu.make_async_remote_copy(
+                src_ref=low.at[direction],
+                dst_ref=gathered.at[direction, mine],
+                send_sem=ag_send.at[direction, o],
+                recv_sem=ag_recv.at[direction, o],
+                device_id={"space": lax.rem(me + o, n)},
+                device_id_type=MESH,
+            )
+            copy.start()
+            sends.append(copy)
+        return sends
+
+    def unpack(direction, sends):
+        for copy in sends:
+            copy.wait_recv()
+        whole = gathered[direction].astype(jnp.float32)
+        flipped = whole.T
+        elem_ref[direction, 0] = jnp.where(
+            row < col, whole, jnp.where(row > col, -flipped, 0.0)
+        ).astype(jnp.bfloat16)
+        elem_ref[direction, 1] = jnp.where(row < col, flipped, whole).astype(jnp.bfloat16)
+
+    own = lambda ri, c: v_ref[ri, c]
+    scattered = {}
+    for direction, which in ((0, 0), (2, 1)):
+        for ri in range(2):
+            for c in range(3):
+                shifted[ri, c] = jnp.dot(
+                    v_ref[ri, c], perm_ref[which], preferred_element_type=jnp.float32
+                ).astype(jnp.bfloat16)
+        mix(link_ref, direction, False, (0, sites), lambda ri, c, rows: shifted[ri, c, rows, :], mixed)
+        scattered[direction] = scatter(direction, *overlap(own, lambda ri, c: mixed[ri, c]))
+
+    down.wait_recv()
+    mix(link_ref, 1, False, (0, split), lambda ri, c, rows: down_in[ri, c, rows, :], mixed_lo)
+    real, imag = overlap(lambda ri, c: v_ref[ri, c, :, 0:split], lambda ri, c: mixed_lo[ri, c])
+    up.wait_recv()
+    real_up, imag_up = overlap(lambda ri, c: up_in[ri, c], lambda ri, c: v_ref[ri, c, :, split:sites])
+    scattered[1] = scatter(1, real + real_up, imag + imag_up)
+
+    sent = {direction: gather(direction, scattered[direction]) for direction in (0, 2, 1)}
+    for direction in (0, 2, 1):
+        unpack(direction, sent[direction])
+    swap.wait()
+    down.wait_send()
+    up.wait_send()
+    for direction in range(3):
+        for copy in scattered[direction] + sent[direction]:
+            copy.wait_send()
+
+
+def shift_tables():
+    site = np.arange(LX * LZ)
+    x, z = site // LZ, site % LZ
+    tables = []
+    for source in (((x + 1) % LX) * LZ + z, x * LZ + (z + 1) % LZ):
+        tables.append(site[:, None] == source[None, :])
+    return jnp.asarray(np.stack(tables), jnp.bfloat16)
+
+
+def exchange(eigvecs, links, peram):
+    n = lax.axis_size("space")
+    sites = LX * LZ
+    bf, chunk = jnp.bfloat16, K // n
+    vmem = pl.BlockSpec(memory_space=pltpu.VMEM)
+    hbm = pl.BlockSpec(memory_space=pl.ANY)
+    return pl.pallas_call(
+        functools.partial(halo_kernel, n),
+        out_shape=(
+            jax.ShapeDtypeStruct((3, 2, K, K), bf),
+            jax.ShapeDtypeStruct(peram.shape[1:], bf),
+        ),
+        in_specs=[vmem, vmem, vmem, hbm],
+        out_specs=(vmem, hbm),
+        scratch_shapes=[
+            pltpu.VMEM((2, 3, K, sites), bf),
+            pltpu.VMEM((2, 3, K, sites), bf),
+            pltpu.VMEM((2, 3, K, 128), bf),
+            pltpu.VMEM((2, 3, K, sites - 128), bf),
+            pltpu.VMEM((2, 3, K, sites - 128), bf),
+            pltpu.VMEM((2, 3, K, 128), bf),
+            pltpu.VMEM((3, K, K), bf),
+            pltpu.VMEM((3, K, K), bf),
+            pltpu.VMEM((3, chunk, K), bf),
+            pltpu.VMEM((3, n, chunk, K), bf),
+            pltpu.SemaphoreType.DMA((3,)),
+            pltpu.SemaphoreType.DMA((3,)),
+            pltpu.SemaphoreType.DMA((3, n)),
+            pltpu.SemaphoreType.DMA((3, n)),
+            pltpu.SemaphoreType.DMA((3, n)),
+            pltpu.SemaphoreType.DMA((3, n)),
+        ],
+        compiler_params=pltpu.CompilerParams(
+            collective_id=0, has_side_effects=True, vmem_limit_bytes=40 * 2**20
+        ),
+    )(
+        jnp.transpose(eigvecs[0], (0, 2, 1, 3)),
+        links[0].reshape(54, sites).astype(jnp.float32),
+        shift_tables(),
+        peram[0],
+    )
+
+
+def on_device(eigvecs, links, dirs, peram):
+    if halo_plan(eigvecs):
+        elem, swapped = exchange(eigvecs, links, peram)
+        picked = [
+            jnp.where(dirs[j] == 0, elem[0], jnp.where(dirs[j] == 1, elem[1], elem[2]))
+            for j in range(3)
+        ]
+        return finish(jnp.stack(picked)[None], swapped[None])
+    return general(eigvecs, links, dirs, peram)
+
+
 def solution(mesh):
     placed = (
         P(("parts", "tm"), None, None, None, "space"),

time: 129 us -> 53.2 us (0.41)
  blocking collectives: 80.4 us -> 0 us
  Pallas kernels: 0 us -> 40 us
  other arithmetic: 19.6 us -> 0.31 us
  starting transfers between devices: 5.98 us -> 0 us
  waiting for transfers between devices: 5.74 us -> 0 us
  local copies, waits for them, and re-layouts: 10.9 us -> 7.21 us
  matrix products: 5.25 us -> 1.6 us
  between operations: 1.09 us -> 3.8 us
    psum x1 -> x0, blocking collectives: 80.4 us -> none  [on_device(): elem_low = lax.psum(stacked, 'space').astype(jnp.bfloat16)]
    pallas_call x0 -> x1, Pallas kernels: none -> 40 us  [exchange(): pl.pallas_call(functools.partial(halo_kernel, n), out_shape=(jax.ShapeDty...]
    another operation x22 -> x1, other arithmetic: 7.29 us -> 0.15 us  [finish(): combined = jnp.stack([out_real, out_imag], axis=1)]
    ppermute x3 -> x0, starting transfers between devices: 5.98 us -> none  [from_behind(): return lax.ppermute(block, axis, route)]
    ppermute x3 -> x0, waiting for transfers between devices: 5.74 us -> none  [from_behind(): return lax.ppermute(block, axis, route)]
    convert_element_type x9 -> x0, other arithmetic: 3.86 us -> none  [the longest x3 1.95 us: on_device(): derivative = (link_apply(link_set[direction], ahead_field, False) - behin...]
    sub x8 -> x0, other arithmetic: 3.79 us -> none  [link_apply(): real_sum = real_sum + link_real * vec_real - link_imag * vec_imag]
    dot_general x16 -> x4, matrix products: 5.25 us -> 1.6 us  [the longest x1 0.4 us: finish(): jnp.einsum('jkl,cls->jcks', elem_imag, peram_imag, preferred_element_type...]
  transfers between devices with their start and end apart: 3 -> 0, of which waited for: 1 -> 0; matrix products, arithmetic and copies ran while one was open for 17% -> 0% of each run, Pallas kernels for 0% -> 0%
where the time goes in v1:
time: 53.2 us; the launch traced here: 52.9 us
  Pallas kernels  40 us (75%)
  local copies, waits for them, and re-layouts  7.21 us (14%)
  between operations  3.8 us (7%)
  matrix products  1.6 us (3%)
    pallas_call x1, Pallas kernels, exchange(): pl.pallas_call(functools.partial(halo_kernel, n), out_shape=(jax.ShapeDty...  40 us
    another operation x1, local copies, waits for them, and re-layouts, finish(): combined = jnp.stack([out_real, out_imag], axis=1)  1.57 us
    slice x1, local copies, waits for them, and re-layouts, on_device(): dirs[j] == 0  1.4 us
    unnamed x5, local copies, waits for them, and re-layouts  1.37 us

profile of v1, /device:TPU:0, one launch (start us, length us, event | category | flops | bytes accessed | tf_op | source)
XLA Modules:
  0.0 52.9 jit_solution(5615381441694664321)
XLA Ops:
  0.0 0.0 copy-start.1
  0.0 0.0 copy-start
  0.0 1.4 %fusion.5 = (s32[1]{0:T(128)}, s32[1]{0:T(128)}, s32[1]{0:T(128)}) fusion(s32[3]{0:T(128)} %param.7), kind=kLoop, calls=%fused_computation.14 | loop fusion | bytes 24 | tf_op jit(solution)/shard_map/slice | solution.py:363
  5.1 0.8 %reshape.52.link_ref = f32[54,216]{1,0:T(8,128)S(1)} reshape(bf16[1,3,3,3,2,216]{5,4,3,2,1,0:T(2,128)(2,1)} %param.6) | data formatting | bytes 69984 | tf_op jit(solution)/shard_map/convert_element_type | solution.py:353
  5.9 1.4 %copy.11 = bf16[1,2,256,3,216]{4,2,3,1,0:T(8,128)(2,1)S(1)} copy(bf16[1,2,256,3,216]{2,4,3,1,0:T(8,128)(2,1)} %param.5) | data formatting | bytes 1327104 | tf_op args[0]
  7.2 0.0 copy-done.1
  7.2 0.0 copy-done
  7.3 40.0 %shard_map.55 = (bf16[3,2,256,256]{3,2,1,0:T(8,128)(2,1)S(1)}, bf16[2,128,1024]{2,1,0:T(8,128)(2,1)S(1)}) custom-call(bf16[2,3,256,216]{3,2,1,0:T(8,128)(2,1)S(1)} %bitcast.43, f32[54,216]{1,0:T(8,128)S(1)} %reshape.52.link_ref, bf16[2,216,216]{2,1,0:T(8,128)(2,1)S(1)} %copy-done.1, bf16[2,128,1024]{2,1,0:T(8,128)(2,1)S(1)} %bitcast.44), custom_call_target="tpu_custom_call" | custom-call | tf_op jit(solution)/shard_map/pallas_call | solution.py:322
  47.3 0.2 copy.12
  47.5 0.2 copy.21
  47.6 0.2 copy.14
  47.8 0.2 copy.22
  48.0 0.1 select_select_fusion.2
  48.1 0.1 maximum_bitcast_fusion
  48.2 0.4 fusion.2
  48.6 0.4 fusion.1
  49.0 0.7 %copy.19 = bf16[3,128,256,4]{1,3,2,0:T(4,128)(2,1)S(1)} copy(bf16[3,128,256,4]{2,1,0,3:T(8,128)(2,1)S(1)} %fusion.1) | data formatting | bytes 1572864 | tf_op jit(solution)/shard_map/add | solution.py:121
  49.7 0.4 fusion.3
  50.1 0.4 fusion
  50.5 0.7 %copy.16 = bf16[3,128,256,4]{1,3,2,0:T(4,128)(2,1)S(1)} copy(bf16[3,128,256,4]{2,1,0,3:T(8,128)(2,1)S(1)} %fusion) | data formatting | bytes 1572864 | tf_op jit(solution)/shard_map/sub | solution.py:118
  51.2 0.1 pad_maximum_fusion
  51.3 1.6 %copy.20 = bf16[1,3,2,128,1024]{4,3,2,1,0:T(8,128)(2,1)} copy(bf16[1,3,2,128,1024]{3,4,1,2,0:T(8,128)(2,1)S(1)} %pad_maximum_fusion) | data formatting | bytes 3145728 | tf_op jit(solution)/shard_map/stack | solution.py:124
  (1 shorter events, 0.0 us)
Async XLA Ops:
  0.0 7.2 %copy-start.1 = (bf16[2,216,216]{2,1,0:T(8,128)(2,1)S(1)}, bf16[2,216,216]{2,1,0:T(8,128)(2,1)}, u32[]{:S(2)}) copy-start(bf16[2,216,216]{2,1,0:T(8,128)(2,1)} %constant.12.clone.perm_ref) | copy-start | bytes 559876
  0.0 7.2 %copy-start = (bf16[1,2,128,1024]{3,2,1,0:T(8,128)(2,1)S(1)}, bf16[1,2,128,1024]{3,2,1,0:T(8,128)(2,1)}, u32[]{:S(2)}) copy-start(bf16[1,2,128,1024]{3,2,1,0:T(8,128)(2,1)} %param.8) | copy-start | bytes 1572868

commit v2 on v1

--- a/solution.py
+++ b/solution.py
@@ -137,20 +137,18 @@
     )
 
 
-def mix(link_ref, direction, adjoint, lanes, source, target):
-    lo, hi = lanes
-
-    @pl.loop(0, K // 16)
-    def _(step):
-        rows = pl.ds(pl.multiple_of(step * 16, 16), 16)
+def mix(link_ref, direction, adjoint, first, count, source, target):
+    def block(start, size):
+        rows = pl.ds(start, size)
+        sites = pl.ds(start + first, size)
         vec = [[source(ri, c, rows).astype(jnp.float32) for c in range(3)] for ri in range(2)]
         for out_row in range(3):
             real_sum = None
             for in_col in range(3):
                 a, b = (in_col, out_row) if adjoint else (out_row, in_col)
                 at = ((direction * 3 + a) * 3 + b) * 2
-                link_real = link_ref[at : at + 1, lo:hi]
-                link_imag = link_ref[at + 1 : at + 2, lo:hi]
+                link_real = link_ref[sites, at : at + 1]
+                link_imag = link_ref[sites, at + 1 : at + 2]
                 rr = link_real * vec[0][in_col]
                 ii = link_imag * vec[1][in_col]
                 ri = link_real * vec[1][in_col]
@@ -162,28 +160,41 @@
             target[0, out_row, rows, :] = real_sum.astype(jnp.bfloat16)
             target[1, out_row, rows, :] = imag_sum.astype(jnp.bfloat16)
 
+    @pl.loop(0, count // 16)
+    def _(step):
+        block(pl.multiple_of(step * 16, 16), 16)
+
+    if count % 16:
+        block(count - count % 16, count % 16)
+
+
+def meet(left, right):
+    return lax.dot_general(
+        left, right, (((0,), (0,)), ((), ())), preferred_element_type=jnp.float32
+    )
+
 
 def overlap(left, right):
     real = imag = None
     for c in range(3):
         lr, li, rr, ri = left(0, c), left(1, c), right(0, c), right(1, c)
-        re = contract(lr, rr) + contract(li, ri)
-        im = contract(lr, ri) - contract(li, rr)
+        re = meet(lr, rr) + meet(li, ri)
+        im = meet(lr, ri) - meet(li, rr)
         real = re if real is None else real + re
         imag = im if imag is None else imag + im
     return real, imag
 
 
 def halo_kernel(
-    n, v_ref, link_ref, perm_ref, peram_ref, elem_ref, swapped_ref,
-    shifted, mixed, mixed_lo, up_out, up_in, down_in, part, gathered, low, landed,
+    n, v_ref, link_ref, perm_ref, peram_ref, elem_ref, spread_ref,
+    shifted, mixed, mixed_lo, up_out, up_in, down_in, part, gathered, low, landed, swapped,
     halo_send, halo_recv, rs_send, rs_recv, ag_send, ag_recv,
 ):
     me = lax.axis_index("space")
     core = lax.axis_index("tm")
     chunk = K // n
-    split = 128
     sites = LX * LZ
+    split = upper_rows(sites)
 
     barrier = pltpu.get_barrier_semaphore()
     for o in range(1, n):
@@ -194,7 +205,7 @@
     pl.semaphore_wait(barrier, n)
 
     down = pltpu.make_async_remote_copy(
-        src_ref=v_ref.at[:, :, :, pl.ds(0, split)],
+        src_ref=v_ref.at[:, :, pl.ds(0, split)],
         dst_ref=down_in,
         send_sem=halo_send.at[0],
         recv_sem=halo_recv.at[0],
@@ -202,7 +213,10 @@
         device_id_type=MESH,
     )
     down.start()
-    mix(link_ref, 1, True, (split, sites), lambda ri, c, rows: v_ref[ri, c, rows, split:sites], up_out)
+    mix(
+        link_ref, 1, True, split, sites - split,
+        lambda ri, c, rows: v_ref[ri, c, pl.ds(rows.start + split, rows.size)], up_out,
+    )
     up = pltpu.make_async_remote_copy(
         src_ref=up_out,
         dst_ref=up_in,
@@ -214,7 +228,7 @@
     up.start()
     swap = pltpu.make_async_remote_copy(
         src_ref=peram_ref,
-        dst_ref=swapped_ref,
+        dst_ref=swapped,
         send_sem=halo_send.at[2],
         recv_sem=halo_recv.at[2],
         device_id={"tm": 1 - core},
@@ -265,38 +279,48 @@
             sends.append(copy)
         return sends
 
-    def unpack(direction, sends):
+    def keep(direction, sends):
         for copy in sends:
             copy.wait_recv()
-        whole = gathered[direction].astype(jnp.float32)
-        flipped = whole.T
-        elem_ref[direction, 0] = jnp.where(
-            row < col, whole, jnp.where(row > col, -flipped, 0.0)
-        ).astype(jnp.bfloat16)
-        elem_ref[direction, 1] = jnp.where(row < col, flipped, whole).astype(jnp.bfloat16)
+        elem_ref[direction] = gathered[direction]
 
     own = lambda ri, c: v_ref[ri, c]
-    scattered = {}
+    scattered, sent = {}, {}
     for direction, which in ((0, 0), (2, 1)):
         for ri in range(2):
             for c in range(3):
                 shifted[ri, c] = jnp.dot(
-                    v_ref[ri, c], perm_ref[which], preferred_element_type=jnp.float32
+                    perm_ref[which], v_ref[ri, c], preferred_element_type=jnp.float32
                 ).astype(jnp.bfloat16)
-        mix(link_ref, direction, False, (0, sites), lambda ri, c, rows: shifted[ri, c, rows, :], mixed)
+        mix(link_ref, direction, False, 0, sites, lambda ri, c, rows: shifted[ri, c, rows], mixed)
         scattered[direction] = scatter(direction, *overlap(own, lambda ri, c: mixed[ri, c]))
 
+    swap.wait()
+    order = spin_order(True)
+    columns = swapped.shape[1]
+    for ri in range(2):
+        for b in range(SPIN):
+            sorted_block = jnp.dot(
+                swapped[ri, :, b * K : (b + 1) * K], order, preferred_element_type=jnp.float32
+            ).astype(jnp.bfloat16)
+            for spin in range(SPIN):
+                at = ri * K + b * (K // SPIN)
+                spread_ref[spin * columns : (spin + 1) * columns, at : at + K // SPIN] = sorted_block[
+                    :, spin * (K // SPIN) : (spin + 1) * (K // SPIN)
+                ]
+    for direction in (0, 2):
+        sent[direction] = gather(direction, scattered[direction])
+
     down.wait_recv()
-    mix(link_ref, 1, False, (0, split), lambda ri, c, rows: down_in[ri, c, rows, :], mixed_lo)
-    real, imag = overlap(lambda ri, c: v_ref[ri, c, :, 0:split], lambda ri, c: mixed_lo[ri, c])
+    mix(link_ref, 1, False, 0, split, lambda ri, c, rows: down_in[ri, c, rows], mixed_lo)
+    real, imag = overlap(lambda ri, c: v_ref[ri, c, 0:split], lambda ri, c: mixed_lo[ri, c])
     up.wait_recv()
-    real_up, imag_up = overlap(lambda ri, c: up_in[ri, c], lambda ri, c: v_ref[ri, c, :, split:sites])
+    real_up, imag_up = overlap(lambda ri, c: up_in[ri, c], lambda ri, c: v_ref[ri, c, split:sites])
     scattered[1] = scatter(1, real + real_up, imag + imag_up)
-
-    sent = {direction: gather(direction, scattered[direction]) for direction in (0, 2, 1)}
-    for direction in (0, 2, 1):
-        unpack(direction, sent[direction])
-    swap.wait()
+    for direction in (0, 2):
+        keep(direction, sent[direction])
+    sent[1] = gather(1, scattered[1])
+    keep(1, sent[1])
     down.wait_send()
     up.wait_send()
     for direction in range(3):
@@ -304,40 +328,99 @@
             copy.wait_send()
 
 
+def spin_order(apart):
+    near = lax.broadcasted_iota(jnp.int32, (K, K), 0 if apart else 1)
+    far = lax.broadcasted_iota(jnp.int32, (K, K), 1 if apart else 0)
+    part = K // SPIN
+    spin = near & (SPIN - 1)
+    hit = far * SPIN == spin * (part * SPIN - 1) + near
+    return jnp.where(hit, 1.0, 0.0).astype(jnp.bfloat16)
+
+
+def upper_rows(sites):
+    return (sites + 31) // 32 * 16
+
+
+def finish_kernel(dirs_ref, elem_ref, spread_ref, out_ref):
+    columns = out_ref.shape[2]
+    part = K // SPIN
+    row = lax.broadcasted_iota(jnp.int32, (K, K), 0)
+    col = lax.broadcasted_iota(jnp.int32, (K, K), 1)
+    back = spin_order(False)
+    packed = elem_ref[dirs_ref[pl.program_id(0)]].astype(jnp.float32)
+    flipped = packed.T
+    minus_real = jnp.where(row < col, -packed, jnp.where(row > col, flipped, 0.0)).astype(jnp.bfloat16)
+    imag = jnp.where(row < col, flipped, packed)
+    minus_imag = (-imag).astype(jnp.bfloat16)
+    imag = imag.astype(jnp.bfloat16)
+    for ri, (first, second) in enumerate(((minus_real, minus_imag), (imag, minus_real))):
+        result = jnp.dot(
+            spread_ref[...], jnp.concatenate([first, second], axis=0), preferred_element_type=jnp.float32
+        ).astype(jnp.bfloat16)
+        for b in range(SPIN):
+            block = jnp.concatenate(
+                [
+                    result[spin * columns : (spin + 1) * columns, b * part : (b + 1) * part]
+                    for spin in range(SPIN)
+                ],
+                axis=1,
+            )
+            out_ref[0, ri, :, b * K : (b + 1) * K] = jnp.dot(
+                block, back, preferred_element_type=jnp.float32
+            ).astype(jnp.bfloat16)
+
+
+def finish_packed(dirs, elem, spread, columns):
+    return pl.pallas_call(
+        finish_kernel,
+        grid=(3,),
+        out_shape=jax.ShapeDtypeStruct((3, 2, columns, K * SPIN), jnp.bfloat16),
+        in_specs=[
+            pl.BlockSpec(memory_space=pltpu.SMEM),
+            pl.BlockSpec((3, K, K), lambda j: (0, 0, 0)),
+            pl.BlockSpec((SPIN * columns, 2 * K), lambda j: (0, 0)),
+        ],
+        out_specs=pl.BlockSpec((1, 2, columns, K * SPIN), lambda j: (j, 0, 0, 0)),
+        compiler_params=pltpu.CompilerParams(vmem_limit_bytes=40 * 2**20),
+    )(dirs, elem, spread)
+
+
 def shift_tables():
     site = np.arange(LX * LZ)
     x, z = site // LZ, site % LZ
     tables = []
     for source in (((x + 1) % LX) * LZ + z, x * LZ + (z + 1) % LZ):
-        tables.append(site[:, None] == source[None, :])
+        tables.append(source[:, None] == site[None, :])
     return jnp.asarray(np.stack(tables), jnp.bfloat16)
 
 
 def exchange(eigvecs, links, peram):
     n = lax.axis_size("space")
     sites = LX * LZ
+    split = upper_rows(sites)
+    columns = peram.shape[2]
     bf, chunk = jnp.bfloat16, K // n
     vmem = pl.BlockSpec(memory_space=pltpu.VMEM)
-    hbm = pl.BlockSpec(memory_space=pl.ANY)
     return pl.pallas_call(
         functools.partial(halo_kernel, n),
         out_shape=(
-            jax.ShapeDtypeStruct((3, 2, K, K), bf),
-            jax.ShapeDtypeStruct(peram.shape[1:], bf),
+            jax.ShapeDtypeStruct((3, K, K), bf),
+            jax.ShapeDtypeStruct((SPIN * columns, 2 * K), bf),
         ),
-        in_specs=[vmem, vmem, vmem, hbm],
-        out_specs=(vmem, hbm),
+        in_specs=[vmem] * 4,
+        out_specs=(vmem, vmem),
         scratch_shapes=[
-            pltpu.VMEM((2, 3, K, sites), bf),
-            pltpu.VMEM((2, 3, K, sites), bf),
-            pltpu.VMEM((2, 3, K, 128), bf),
-            pltpu.VMEM((2, 3, K, sites - 128), bf),
-            pltpu.VMEM((2, 3, K, sites - 128), bf),
-            pltpu.VMEM((2, 3, K, 128), bf),
+            pltpu.VMEM((2, 3, sites, K), bf),
+            pltpu.VMEM((2, 3, sites, K), bf),
+            pltpu.VMEM((2, 3, split, K), bf),
+            pltpu.VMEM((2, 3, sites - split, K), bf),
+            pltpu.VMEM((2, 3, sites - split, K), bf),
+            pltpu.VMEM((2, 3, split, K), bf),
             pltpu.VMEM((3, K, K), bf),
             pltpu.VMEM((3, K, K), bf),
             pltpu.VMEM((3, chunk, K), bf),
             pltpu.VMEM((3, n, chunk, K), bf),
+            pltpu.VMEM(peram.shape[1:], bf),
             pltpu.SemaphoreType.DMA((3,)),
             pltpu.SemaphoreType.DMA((3,)),
             pltpu.SemaphoreType.DMA((3, n)),
@@ -349,8 +432,8 @@
             collective_id=0, has_side_effects=True, vmem_limit_bytes=40 * 2**20
         ),
     )(
-        jnp.transpose(eigvecs[0], (0, 2, 1, 3)),
-        links[0].reshape(54, sites).astype(jnp.float32),
+        jnp.transpose(eigvecs[0], (0, 2, 3, 1)),
+        links[0].reshape(54, sites).T.astype(jnp.float32),
         shift_tables(),
         peram[0],
     )
@@ -358,12 +441,8 @@
 
 def on_device(eigvecs, links, dirs, peram):
     if halo_plan(eigvecs):
-        elem, swapped = exchange(eigvecs, links, peram)
-        picked = [
-            jnp.where(dirs[j] == 0, elem[0], jnp.where(dirs[j] == 1, elem[1], elem[2]))
-            for j in range(3)
-        ]
-        return finish(jnp.stack(picked)[None], swapped[None])
+        elem, spread = exchange(eigvecs, links, peram)
+        return finish_packed(dirs, elem, spread, peram.shape[2])[None]
     return general(eigvecs, links, dirs, peram)
 
 

time: 53.2 us -> 49.4 us (0.929)
  Pallas kernels: 40 us -> 45.1 us
  between operations: 3.8 us -> 0.03 us
  local copies, waits for them, and re-layouts: 7.21 us -> 3.97 us
  matrix products: 1.6 us -> 0 us
    pallas_call x0 -> x1, Pallas kernels: none -> 5.54 us  [finish_packed(): pl.pallas_call(finish_kernel, grid=(3,), out_shape=jax.ShapeDtypeStruct((...]
    another operation x3 -> x0, local copies, waits for them, and re-layouts: 1.93 us -> none  [the longest x1 1.57 us: finish(): combined = jnp.stack([out_real, out_imag], axis=1)]
    slice x4 -> x0, local copies, waits for them, and re-layouts: 1.77 us -> none  [the longest x1 1.4 us: on_device(): dirs[j] == 0]
    unnamed x5 -> x8, local copies, waits for them, and re-layouts: 1.37 us -> 3.06 us
    dot_general x4 -> x0, matrix products: 1.6 us -> none  [the longest x1 0.4 us: finish(): jnp.einsum('jkl,cls->jcks', elem_imag, peram_imag, preferred_element_type...]
    add x1 -> x0, local copies, waits for them, and re-layouts: 0.68 us -> none  [finish(): jnp.einsum('jkl,cls->jcks', elem_real, peram_imag, preferred_element_type...]
    sub x1 -> x0, local copies, waits for them, and re-layouts: 0.68 us -> none  [finish(): jnp.einsum('jkl,cls->jcks', elem_real, peram_real, preferred_element_type...]
where the time goes in v2:
time: 49.4 us; the launch traced here: 49.1 us
  Pallas kernels  45.1 us (91%)
  local copies, waits for them, and re-layouts  3.97 us (8%)
    pallas_call x1, Pallas kernels, exchange(): pl.pallas_call(functools.partial(halo_kernel, n), out_shape=(jax.ShapeDty...  39.6 us
    pallas_call x1, Pallas kernels, finish_packed(): pl.pallas_call(finish_kernel, grid=(3,), out_shape=jax.ShapeDtypeStruct((...  5.54 us
    unnamed x8, local copies, waits for them, and re-layouts  3.06 us

profile of v2, /device:TPU:0, one launch (start us, length us, event | category | flops | bytes accessed | tf_op | source)
XLA Modules:
  0.0 49.1 jit_solution(12012757296102635426)
XLA Ops:
  0.0 0.0 copy-start.3
  0.0 0.8 %reshape.2 = f32[54,216]{1,0:T(8,128)S(1)} reshape(bf16[1,3,3,3,2,216]{5,4,3,2,1,0:T(2,128)(2,1)} %param.6) | data formatting | bytes 69984 | tf_op jit(solution)/shard_map/convert_element_type | solution.py:436
  0.8 0.1 copy.7
  0.9 0.0 copy-start
  0.9 1.1 %copy-done = bf16[1,2,256,3,216]{2,4,3,1,0:T(8,128)(2,1)S(1)} copy-done((bf16[1,2,256,3,216]{2,4,3,1,0:T(8,128)(2,1)S(1)}, bf16[1,2,256,3,216]{2,4,3,1,0:T(8,128)(2,1)}, u32[]{:S(2)}) %copy-start) | copy-done | bytes 663576
  2.0 0.0 copy-start.1
  2.0 1.0 %copy-done.1 = bf16[1,2,128,1024]{3,2,1,0:T(8,128)(2,1)S(1)} copy-done((bf16[1,2,128,1024]{3,2,1,0:T(8,128)(2,1)S(1)}, bf16[1,2,128,1024]{3,2,1,0:T(8,128)(2,1)}, u32[]{:S(2)}) %copy-start.1) | copy-done | bytes 524312
  3.0 0.0 copy-start.2
  3.0 0.9 %copy-done.2 = bf16[2,216,216]{2,1,0:T(8,128)(2,1)S(1)} copy-done((bf16[2,216,216]{2,1,0:T(8,128)(2,1)S(1)}, bf16[2,216,216]{2,1,0:T(8,128)(2,1)}, u32[]{:S(2)}) %copy-start.2) | copy-done | bytes 186648
  4.0 39.6 %shard_map.55 = (bf16[3,256,256]{2,1,0:T(8,128)(2,1)S(1)}, bf16[512,512]{1,0:T(8,128)(2,1)S(1)}) custom-call(bf16[2,3,216,256]{3,2,1,0:T(8,128)(2,1)S(1)} %bitcast.6, f32[216,54]{1,0:T(8,128)S(1)} %bitcast.8, bf16[2,216,216]{2,1,0:T(8,128)(2,1)S(1)} %copy-done.2, bf16[2,128,1024]{2,1,0:T(8,128)(2,1)S(1)} %bitcast.7), custom_call_target="tpu_custom_call" | custom-call | tf_op jit(solution)/shard_map/pallas_call | solution.py:404
  43.6 0.0 copy-done.3
  43.6 5.5 %shard_map.56 = bf16[3,2,128,1024]{3,2,1,0:T(8,128)(2,1)} custom-call(s32[3]{0:T(128)S(1)} %copy-done.3, bf16[3,256,256]{2,1,0:T(8,128)(2,1)S(1)} %get-tuple-element.7.elem_ref, bf16[512,512]{1,0:T(8,128)(2,1)S(1)} %get-tuple-element.8.spread_ref), custom_call_target="tpu_custom_call" | custom-call | tf_op jit(solution)/shard_map/pallas_call | solution.py:374
Async XLA Ops:
  0.0 43.6 %copy-start.3 = (s32[3]{0:T(128)S(1)}, s32[3]{0:T(128)}, u32[]{:S(2)}) copy-start(s32[3]{0:T(128)} %dirs_ref.1) | copy-start | bytes 40
  0.9 1.1 %copy-start = (bf16[1,2,256,3,216]{2,4,3,1,0:T(8,128)(2,1)S(1)}, bf16[1,2,256,3,216]{2,4,3,1,0:T(8,128)(2,1)}, u32[]{:S(2)}) copy-start(bf16[1,2,256,3,216]{2,4,3,1,0:T(8,128)(2,1)} %param.5) | copy-start | bytes 1990660
  2.0 1.0 %copy-start.1 = (bf16[1,2,128,1024]{3,2,1,0:T(8,128)(2,1)S(1)}, bf16[1,2,128,1024]{3,2,1,0:T(8,128)(2,1)}, u32[]{:S(2)}) copy-start(bf16[1,2,128,1024]{3,2,1,0:T(8,128)(2,1)} %param.8) | copy-start | bytes 1572868
  3.0 0.9 %copy-start.2 = (bf16[2,216,216]{2,1,0:T(8,128)(2,1)S(1)}, bf16[2,216,216]{2,1,0:T(8,128)(2,1)}, u32[]{:S(2)}) copy-start(bf16[2,216,216]{2,1,0:T(8,128)(2,1)} %constant.2.clone.perm_ref) | copy-start | bytes 559876

commit v3 on v2

--- a/solution.py
+++ b/solution.py
@@ -2,7 +2,6 @@
 
 import jax
 import jax.numpy as jnp
-import numpy as np
 from jax import lax
 from jax.experimental import pallas as pl
 from jax.experimental.pallas import tpu as pltpu
@@ -131,7 +130,7 @@
     return (
         eigvecs.shape[-1] == LX * LZ
         and lax.axis_size("tm") == 2
-        and n > 1
+        and n % 2 == 0
         and eigvecs.shape[0] == 1
         and K % (16 * n) == 0
     )
@@ -186,9 +185,9 @@
 
 
 def halo_kernel(
-    n, v_ref, link_ref, perm_ref, peram_ref, elem_ref, spread_ref,
-    shifted, mixed, mixed_lo, up_out, up_in, down_in, part, gathered, low, landed, swapped,
-    halo_send, halo_recv, rs_send, rs_recv, ag_send, ag_recv,
+    n, v_hbm, link_ref, peram_hbm, elem_ref, spread_ref, v_ref, tables,
+    shifted, mixed, mixed_lo, up_out, up_in, down_in, part, gathered, low, landed, landed_levels, landed_pair, quarters, swapped,
+    load_sem, halo_send, halo_recv, rs_send, rs_recv, ag_send, ag_recv,
 ):
     me = lax.axis_index("space")
     core = lax.axis_index("tm")
@@ -196,6 +195,8 @@
     sites = LX * LZ
     split = upper_rows(sites)
 
+    load = pltpu.make_async_copy(v_hbm, v_ref, load_sem)
+    load.start()
     barrier = pltpu.get_barrier_semaphore()
     for o in range(1, n):
         pl.semaphore_signal(
@@ -205,7 +206,7 @@
     pl.semaphore_wait(barrier, n)
 
     down = pltpu.make_async_remote_copy(
-        src_ref=v_ref.at[:, :, pl.ds(0, split)],
+        src_ref=v_hbm.at[:, :, pl.ds(0, split)],
         dst_ref=down_in,
         send_sem=halo_send.at[0],
         recv_sem=halo_recv.at[0],
@@ -213,6 +214,7 @@
         device_id_type=MESH,
     )
     down.start()
+    load.wait()
     mix(
         link_ref, 1, True, split, sites - split,
         lambda ri, c, rows: v_ref[ri, c, pl.ds(rows.start + split, rows.size)], up_out,
@@ -227,7 +229,7 @@
     )
     up.start()
     swap = pltpu.make_async_remote_copy(
-        src_ref=peram_ref,
+        src_ref=peram_hbm,
         dst_ref=swapped,
         send_sem=halo_send.at[2],
         recv_sem=halo_recv.at[2],
@@ -239,61 +241,129 @@
     row = lax.broadcasted_iota(jnp.int32, (K, K), 0)
     col = lax.broadcasted_iota(jnp.int32, (K, K), 1)
 
-    def scatter(direction, real, imag):
+    half = lax.rem(me, 2)
+    level = lax.div(me, 2)
+    levels = n // 2
+    pair = me + 1 - 2 * half
+    quarter = 2 * chunk
+
+    def send(src, dst, out_sem, in_sem, peer):
+        copy = pltpu.make_async_remote_copy(
+            src_ref=src, dst_ref=dst, send_sem=out_sem, recv_sem=in_sem,
+            device_id={"space": peer}, device_id_type=MESH,
+        )
+        copy.start()
+        return copy
+
+    def band(index, size):
+        return pl.ds(pl.multiple_of(index * size, size), size)
+
+    def pack(direction, real, imag):
         turned = jnp.where(row > col, -real, imag).T
         part[direction] = (jnp.where(row < col, real, imag) + turned).astype(jnp.bfloat16)
+
+    def scatter(direction):
         copies = []
         for o in range(1, n):
             peer = lax.rem(me + o, n)
-            copy = pltpu.make_async_remote_copy(
-                src_ref=part.at[direction, pl.ds(pl.multiple_of(peer * chunk, chunk), chunk)],
-                dst_ref=landed.at[direction, o],
-                send_sem=rs_send.at[direction, o],
-                recv_sem=rs_recv.at[direction, o],
-                device_id={"space": peer},
-                device_id_type=MESH,
-            )
-            copy.start()
-            copies.append(copy)
+            copies.append(send(
+                part.at[direction, band(peer, chunk)], landed.at[o],
+                rs_send.at[direction, o], rs_recv.at[direction, o], peer,
+            ))
         return copies
 
     def gather(direction, copies):
-        mine = pl.ds(pl.multiple_of(me * chunk, chunk), chunk)
-        total = part[direction, mine].astype(jnp.float32)
+        total = part[direction, band(me, chunk)].astype(jnp.float32)
         for o in range(1, n):
             copies[o - 1].wait_recv()
-            total = total + landed[direction, o].astype(jnp.float32)
+            total = total + landed[o].astype(jnp.float32)
         low[direction] = total.astype(jnp.bfloat16)
-        gathered[direction, mine] = low[direction]
-        sends = []
-        for o in range(1, n):
-            copy = pltpu.make_async_remote_copy(
-                src_ref=low.at[direction],
-                dst_ref=gathered.at[direction, mine],
-                send_sem=ag_send.at[direction, o],
-                recv_sem=ag_recv.at[direction, o],
-                device_id={"space": lax.rem(me + o, n)},
-                device_id_type=MESH,
+        gathered[direction, band(me, chunk)] = low[direction]
+        return [
+            send(
+                low.at[direction], gathered.at[direction, band(me, chunk)],
+                ag_send.at[direction, o], ag_recv.at[direction, o], lax.rem(me + o, n),
             )
-            copy.start()
-            sends.append(copy)
-        return sends
+            for o in range(1, n)
+        ]
+
+    def level_peer(o):
+        to = lax.rem(level + o, levels)
+        return to, to * 2 + half
+
+    def scatter_levels(direction):
+        copies = []
+        for o in range(1, levels):
+            to, peer = level_peer(o)
+            copies.append(send(
+                part.at[direction, band(to, quarter)], landed_levels.at[direction, o],
+                rs_send.at[direction, o], rs_recv.at[direction, o], peer,
+            ))
+        return copies
+
+    def scatter_pair(direction, copies):
+        total = part[direction, band(level, quarter)].astype(jnp.float32)
+        for o in range(1, levels):
+            copies[o - 1].wait_recv()
+            total = total + landed_levels[direction, o].astype(jnp.float32)
+        quarters[direction] = total.astype(jnp.bfloat16)
+        return send(
+            quarters.at[direction, band(1 - half, chunk)], landed_pair.at[direction],
+            rs_send.at[direction, 0], rs_recv.at[direction, 0], pair,
+        )
+
+    def gather_levels(direction, copy):
+        copy.wait_recv()
+        total = quarters[direction, band(half, chunk)].astype(jnp.float32)
+        low[direction] = (total + landed_pair[direction].astype(jnp.float32)).astype(jnp.bfloat16)
+        gathered[direction, band(me, chunk)] = low[direction]
+        copies = [send(
+            low.at[direction], gathered.at[direction, band(me, chunk)],
+            ag_send.at[direction, 0], ag_recv.at[direction, 0], pair,
+        )]
+        for o in range(1, levels):
+            copies.append(send(
+                low.at[direction], gathered.at[direction, band(me, chunk)],
+                ag_send.at[direction, o], ag_recv.at[direction, o], level_peer(o)[1],
+            ))
+        return copies
+
+    def gather_pair(direction, copies):
+        passed = []
+        for o in range(1, levels):
+            copies[o].wait_recv()
+            rows = band(lax.rem(level - o + levels, levels) * 2 + half, chunk)
+            passed.append(send(
+                gathered.at[direction, rows], gathered.at[direction, rows],
+                ag_send.at[direction, levels + o], ag_recv.at[direction, levels + o], pair,
+            ))
+        return copies[:1] + passed
 
     def keep(direction, sends):
         for copy in sends:
             copy.wait_recv()
-        elem_ref[direction] = gathered[direction]
+        packed = gathered[direction].astype(jnp.float32)
+        flipped = packed.T
+        upper = row < col
+        minus_real = jnp.where(upper, -packed, jnp.where(row > col, flipped, 0.0)).astype(jnp.bfloat16)
+        imag = jnp.where(upper, flipped, packed)
+        elem_ref[direction, 0:K, 0:K] = minus_real
+        elem_ref[direction, K : 2 * K, K : 2 * K] = minus_real
+        elem_ref[direction, 0:K, K : 2 * K] = imag.astype(jnp.bfloat16)
+        elem_ref[direction, K : 2 * K, 0:K] = (-imag).astype(jnp.bfloat16)
 
     own = lambda ri, c: v_ref[ri, c]
-    scattered, sent = {}, {}
+    shift_tables(tables, sites)
+    first = {}
     for direction, which in ((0, 0), (2, 1)):
         for ri in range(2):
             for c in range(3):
                 shifted[ri, c] = jnp.dot(
-                    perm_ref[which], v_ref[ri, c], preferred_element_type=jnp.float32
+                    tables[which], v_ref[ri, c], preferred_element_type=jnp.float32
                 ).astype(jnp.bfloat16)
         mix(link_ref, direction, False, 0, sites, lambda ri, c, rows: shifted[ri, c, rows], mixed)
-        scattered[direction] = scatter(direction, *overlap(own, lambda ri, c: mixed[ri, c]))
+        pack(direction, *overlap(own, lambda ri, c: mixed[ri, c]))
+        first[direction] = scatter_levels(direction)
 
     swap.wait()
     order = spin_order(True)
@@ -308,23 +378,27 @@
                 spread_ref[spin * columns : (spin + 1) * columns, at : at + K // SPIN] = sorted_block[
                     :, spin * (K // SPIN) : (spin + 1) * (K // SPIN)
                 ]
-    for direction in (0, 2):
-        sent[direction] = gather(direction, scattered[direction])
+    second = {direction: scatter_pair(direction, first[direction]) for direction in (0, 2)}
 
     down.wait_recv()
     mix(link_ref, 1, False, 0, split, lambda ri, c, rows: down_in[ri, c, rows], mixed_lo)
     real, imag = overlap(lambda ri, c: v_ref[ri, c, 0:split], lambda ri, c: mixed_lo[ri, c])
+    third = {direction: gather_levels(direction, second[direction]) for direction in (0, 2)}
     up.wait_recv()
     real_up, imag_up = overlap(lambda ri, c: up_in[ri, c], lambda ri, c: v_ref[ri, c, split:sites])
-    scattered[1] = scatter(1, real + real_up, imag + imag_up)
+    pack(1, real + real_up, imag + imag_up)
+    scattered = scatter(1)
+    last = {direction: gather_pair(direction, third[direction]) for direction in (0, 2)}
+    sent = gather(1, scattered)
     for direction in (0, 2):
-        keep(direction, sent[direction])
-    sent[1] = gather(1, scattered[1])
-    keep(1, sent[1])
+        keep(direction, last[direction])
+    keep(1, sent)
     down.wait_send()
     up.wait_send()
-    for direction in range(3):
-        for copy in scattered[direction] + sent[direction]:
+    for copy in scattered + sent:
+        copy.wait_send()
+    for direction in (0, 2):
+        for copy in first[direction] + [second[direction]] + third[direction] + last[direction][1:]:
             copy.wait_send()
 
 
@@ -344,30 +418,29 @@
 def finish_kernel(dirs_ref, elem_ref, spread_ref, out_ref):
     columns = out_ref.shape[2]
     part = K // SPIN
-    row = lax.broadcasted_iota(jnp.int32, (K, K), 0)
-    col = lax.broadcasted_iota(jnp.int32, (K, K), 1)
     back = spin_order(False)
-    packed = elem_ref[dirs_ref[pl.program_id(0)]].astype(jnp.float32)
-    flipped = packed.T
-    minus_real = jnp.where(row < col, -packed, jnp.where(row > col, flipped, 0.0)).astype(jnp.bfloat16)
-    imag = jnp.where(row < col, flipped, packed)
-    minus_imag = (-imag).astype(jnp.bfloat16)
-    imag = imag.astype(jnp.bfloat16)
-    for ri, (first, second) in enumerate(((minus_real, minus_imag), (imag, minus_real))):
-        result = jnp.dot(
-            spread_ref[...], jnp.concatenate([first, second], axis=0), preferred_element_type=jnp.float32
-        ).astype(jnp.bfloat16)
-        for b in range(SPIN):
-            block = jnp.concatenate(
+    result = jnp.dot(
+        spread_ref[...], elem_ref[dirs_ref[pl.program_id(0)]], preferred_element_type=jnp.float32
+    ).astype(jnp.bfloat16)
+    stacked = jnp.concatenate(
+        [
+            jnp.concatenate(
                 [
-                    result[spin * columns : (spin + 1) * columns, b * part : (b + 1) * part]
-                    for spin in range(SPIN)
+                    result[s * columns : (s + 1) * columns, ri * K + b * part : ri * K + (b + 1) * part]
+                    for s in range(SPIN)
                 ],
                 axis=1,
             )
-            out_ref[0, ri, :, b * K : (b + 1) * K] = jnp.dot(
-                block, back, preferred_element_type=jnp.float32
-            ).astype(jnp.bfloat16)
+            for ri in range(2)
+            for b in range(SPIN)
+        ],
+        axis=0,
+    )
+    mixed = jnp.dot(stacked, back, preferred_element_type=jnp.float32).astype(jnp.bfloat16)
+    for ri in range(2):
+        for b in range(SPIN):
+            at = (ri * SPIN + b) * columns
+            out_ref[0, ri, :, b * K : (b + 1) * K] = mixed[at : at + columns]
 
 
 def finish_packed(dirs, elem, spread, columns):
@@ -377,21 +450,24 @@
         out_shape=jax.ShapeDtypeStruct((3, 2, columns, K * SPIN), jnp.bfloat16),
         in_specs=[
             pl.BlockSpec(memory_space=pltpu.SMEM),
-            pl.BlockSpec((3, K, K), lambda j: (0, 0, 0)),
-            pl.BlockSpec((SPIN * columns, 2 * K), lambda j: (0, 0)),
+            pl.BlockSpec(memory_space=pltpu.VMEM),
+            pl.BlockSpec(memory_space=pltpu.VMEM),
         ],
         out_specs=pl.BlockSpec((1, 2, columns, K * SPIN), lambda j: (j, 0, 0, 0)),
         compiler_params=pltpu.CompilerParams(vmem_limit_bytes=40 * 2**20),
     )(dirs, elem, spread)
 
 
-def shift_tables():
-    site = np.arange(LX * LZ)
-    x, z = site // LZ, site % LZ
-    tables = []
-    for source in (((x + 1) % LX) * LZ + z, x * LZ + (z + 1) % LZ):
-        tables.append(source[:, None] == site[None, :])
-    return jnp.asarray(np.stack(tables), jnp.bfloat16)
+def shift_tables(tables, sites):
+    here = lax.broadcasted_iota(jnp.int32, (sites, sites), 0)
+    there = lax.broadcasted_iota(jnp.int32, (sites, sites), 1)
+    step = there - here
+    tables[0] = jnp.where((step == LZ) | (step == LZ - sites), 1.0, 0.0).astype(jnp.bfloat16)
+    first = there == 0
+    for x in range(1, LX):
+        first = first | (there == x * LZ)
+    wanted = jnp.where(first, 1 - LZ, 1)
+    tables[1] = jnp.where(step == wanted, 1.0, 0.0).astype(jnp.bfloat16)
 
 
 def exchange(eigvecs, links, peram):
@@ -401,15 +477,18 @@
     columns = peram.shape[2]
     bf, chunk = jnp.bfloat16, K // n
     vmem = pl.BlockSpec(memory_space=pltpu.VMEM)
+    hbm = pl.BlockSpec(memory_space=pltpu.HBM)
     return pl.pallas_call(
         functools.partial(halo_kernel, n),
         out_shape=(
-            jax.ShapeDtypeStruct((3, K, K), bf),
+            jax.ShapeDtypeStruct((3, 2 * K, 2 * K), bf),
             jax.ShapeDtypeStruct((SPIN * columns, 2 * K), bf),
         ),
-        in_specs=[vmem] * 4,
+        in_specs=[hbm, vmem, hbm],
         out_specs=(vmem, vmem),
         scratch_shapes=[
+            pltpu.VMEM((2, 3, sites, K), bf),
+            pltpu.VMEM((2, sites, sites), bf),
             pltpu.VMEM((2, 3, sites, K), bf),
             pltpu.VMEM((2, 3, sites, K), bf),
             pltpu.VMEM((2, 3, split, K), bf),
@@ -419,8 +498,12 @@
             pltpu.VMEM((3, K, K), bf),
             pltpu.VMEM((3, K, K), bf),
             pltpu.VMEM((3, chunk, K), bf),
-            pltpu.VMEM((3, n, chunk, K), bf),
+            pltpu.VMEM((n, chunk, K), bf),
+            pltpu.VMEM((3, n // 2, 2 * chunk, K), bf),
+            pltpu.VMEM((3, chunk, K), bf),
+            pltpu.VMEM((3, 2 * chunk, K), bf),
             pltpu.VMEM(peram.shape[1:], bf),
+            pltpu.SemaphoreType.DMA,
             pltpu.SemaphoreType.DMA((3,)),
             pltpu.SemaphoreType.DMA((3,)),
             pltpu.SemaphoreType.DMA((3, n)),
@@ -434,7 +517,6 @@
     )(
         jnp.transpose(eigvecs[0], (0, 2, 3, 1)),
         links[0].reshape(54, sites).T.astype(jnp.float32),
-        shift_tables(),
         peram[0],
     )
 

time: 49.4 us -> 43.4 us (0.88)
  Pallas kernels: 45.1 us -> 39.4 us
    pallas_call x1, Pallas kernels: 39.6 us -> 35.5 us  [exchange(): pl.pallas_call(functools.partial(halo_kernel, n), out_shape=(jax.ShapeDty...]
    pallas_call x1, Pallas kernels: 5.54 us -> 3.98 us  [finish_packed(): pl.pallas_call(finish_kernel, grid=(3,), out_shape=jax.ShapeDtypeStruct((...]
    unnamed x8 -> x6, local copies, waits for them, and re-layouts: 3.06 us -> 2.77 us
where the time goes in v3:
time: 43.4 us; the launch traced here: 43.1 us
  Pallas kernels  39.4 us (91%)
  local copies, waits for them, and re-layouts  3.66 us (8%)
    pallas_call x1, Pallas kernels, exchange(): pl.pallas_call(functools.partial(halo_kernel, n), out_shape=(jax.ShapeDty...  35.5 us
    pallas_call x1, Pallas kernels, finish_packed(): pl.pallas_call(finish_kernel, grid=(3,), out_shape=jax.ShapeDtypeStruct((...  3.98 us
    unnamed x6, local copies, waits for them, and re-layouts  2.77 us
    convert_element_type x2, local copies, waits for them, and re-layouts, exchange(): links[0].reshape(54, sites).T.astype(jnp.float32)  0.89 us

profile of v3, /device:TPU:0, one launch (start us, length us, event | category | flops | bytes accessed | tf_op | source)
XLA Modules:
  0.0 43.1 jit_solution(5144260583261063750)
XLA Ops:
  0.0 0.8 %reshape.2 = f32[54,216]{1,0:T(8,128)S(1)} reshape(bf16[1,3,3,3,2,216]{5,4,3,2,1,0:T(2,128)(2,1)} %param.5) | data formatting | bytes 69984 | tf_op jit(solution)/shard_map/convert_element_type | solution.py:519
  0.8 0.1 copy.6
  0.9 0.0 copy-start
  0.9 1.1 %copy-done = bf16[1,2,256,3,216]{2,4,3,1,0:T(8,128)(2,1)S(1)} copy-done((bf16[1,2,256,3,216]{2,4,3,1,0:T(8,128)(2,1)S(1)}, bf16[1,2,256,3,216]{2,4,3,1,0:T(8,128)(2,1)}, u32[]{:S(2)}) %copy-start) | copy-done | bytes 663576
  2.0 0.0 copy-start.1
  2.0 1.0 %copy-done.1 = bf16[1,2,128,1024]{3,2,1,0:T(8,128)(2,1)S(1)} copy-done((bf16[1,2,128,1024]{3,2,1,0:T(8,128)(2,1)S(1)}, bf16[1,2,128,1024]{3,2,1,0:T(8,128)(2,1)}, u32[]{:S(2)}) %copy-start.1) | copy-done | bytes 524312
  3.0 35.5 %shard_map.46 = (bf16[3,512,512]{2,1,0:T(8,128)(2,1)S(1)}, bf16[512,512]{1,0:T(8,128)(2,1)S(1)}) custom-call(bf16[2,3,216,256]{3,2,1,0:T(8,128)(2,1)S(1)} %bitcast.6, f32[216,54]{1,0:T(8,128)S(1)} %bitcast.8, bf16[2,128,1024]{2,1,0:T(8,128)(2,1)S(1)} %bitcast.7), custom_call_target="tpu_custom_call" | custom-call | tf_op jit(solution)/shard_map/pallas_call | solution.py:481
  38.5 0.0 copy-start.2
  38.5 0.6 %copy-done.2 = s32[3]{0:T(128)S(1)} copy-done((s32[3]{0:T(128)S(1)}, s32[3]{0:T(128)}, u32[]{:S(2)}) %copy-start.2) | copy-done | bytes 36
  39.2 4.0 %shard_map.47 = bf16[3,2,128,1024]{3,2,1,0:T(8,128)(2,1)} custom-call(s32[3]{0:T(128)S(1)} %copy-done.2, bf16[3,512,512]{2,1,0:T(8,128)(2,1)S(1)} %get-tuple-element.7.elem_ref, bf16[512,512]{1,0:T(8,128)(2,1)S(1)} %get-tuple-element.8.spread_ref), custom_call_target="tpu_custom_call" | custom-call | tf_op jit(solution)/shard_map/pallas_call | solution.py:447
Async XLA Ops:
  0.9 1.1 %copy-start = (bf16[1,2,256,3,216]{2,4,3,1,0:T(8,128)(2,1)S(1)}, bf16[1,2,256,3,216]{2,4,3,1,0:T(8,128)(2,1)}, u32[]{:S(2)}) copy-start(bf16[1,2,256,3,216]{2,4,3,1,0:T(8,128)(2,1)} %param.4) | copy-start | bytes 1990660
  2.0 1.0 %copy-start.1 = (bf16[1,2,128,1024]{3,2,1,0:T(8,128)(2,1)S(1)}, bf16[1,2,128,1024]{3,2,1,0:T(8,128)(2,1)}, u32[]{:S(2)}) copy-start(bf16[1,2,128,1024]{3,2,1,0:T(8,128)(2,1)} %param.7) | copy-start | bytes 1572868
  38.5 0.7 %copy-start.2 = (s32[3]{0:T(128)S(1)}, s32[3]{0:T(128)}, u32[]{:S(2)}) copy-start(s32[3]{0:T(128)} %dirs_ref.1) | copy-start | bytes 40

commit v4 on v3

--- a/solution.py
+++ b/solution.py
@@ -203,6 +203,12 @@
             barrier, inc=1, device_id={"space": lax.rem(me + o, n)}, device_id_type=MESH
         )
     pl.semaphore_signal(barrier, inc=1, device_id={"tm": 1 - core}, device_id_type=MESH)
+    load.wait()
+    mix(
+        link_ref, 1, True, split, sites - split,
+        lambda ri, c, rows: v_ref[ri, c, pl.ds(rows.start + split, rows.size)], up_out,
+    )
+    shift_tables(tables, sites)
     pl.semaphore_wait(barrier, n)
 
     down = pltpu.make_async_remote_copy(
@@ -214,11 +220,6 @@
         device_id_type=MESH,
     )
     down.start()
-    load.wait()
-    mix(
-        link_ref, 1, True, split, sites - split,
-        lambda ri, c, rows: v_ref[ri, c, pl.ds(rows.start + split, rows.size)], up_out,
-    )
     up = pltpu.make_async_remote_copy(
         src_ref=up_out,
         dst_ref=up_in,
@@ -353,7 +354,6 @@
         elem_ref[direction, K : 2 * K, 0:K] = (-imag).astype(jnp.bfloat16)
 
     own = lambda ri, c: v_ref[ri, c]
-    shift_tables(tables, sites)
     first = {}
     for direction, which in ((0, 0), (2, 1)):
         for ri in range(2):

time: 43.4 us -> 43.1 us (level)
  no operation moved by 1% of the time
where the time goes in v4:
time: 43.1 us; the launch traced here: 42.9 us
  Pallas kernels  39.2 us (91%)
  local copies, waits for them, and re-layouts  3.66 us (8%)
    pallas_call x1, Pallas kernels, exchange(): pl.pallas_call(functools.partial(halo_kernel, n), out_shape=(jax.ShapeDty...  35.2 us
    pallas_call x1, Pallas kernels, finish_packed(): pl.pallas_call(finish_kernel, grid=(3,), out_shape=jax.ShapeDtypeStruct((...  3.98 us
    unnamed x6, local copies, waits for them, and re-layouts  2.77 us
    convert_element_type x2, local copies, waits for them, and re-layouts, exchange(): links[0].reshape(54, sites).T.astype(jnp.float32)  0.89 us

profile of v4, /device:TPU:0, one launch (start us, length us, event | category | flops | bytes accessed | tf_op | source)
XLA Modules:
  0.0 42.9 jit_solution(8153245096608125983)
XLA Ops:
  0.0 0.8 %reshape.2 = f32[54,216]{1,0:T(8,128)S(1)} reshape(bf16[1,3,3,3,2,216]{5,4,3,2,1,0:T(2,128)(2,1)} %param.5) | data formatting | bytes 69984 | tf_op jit(solution)/shard_map/convert_element_type | solution.py:519
  0.8 0.1 copy.6
  0.9 0.0 copy-start
  0.9 1.1 %copy-done = bf16[1,2,256,3,216]{2,4,3,1,0:T(8,128)(2,1)S(1)} copy-done((bf16[1,2,256,3,216]{2,4,3,1,0:T(8,128)(2,1)S(1)}, bf16[1,2,256,3,216]{2,4,3,1,0:T(8,128)(2,1)}, u32[]{:S(2)}) %copy-start) | copy-done | bytes 663576
  2.0 0.0 copy-start.1
  2.0 1.0 %copy-done.1 = bf16[1,2,128,1024]{3,2,1,0:T(8,128)(2,1)S(1)} copy-done((bf16[1,2,128,1024]{3,2,1,0:T(8,128)(2,1)S(1)}, bf16[1,2,128,1024]{3,2,1,0:T(8,128)(2,1)}, u32[]{:S(2)}) %copy-start.1) | copy-done | bytes 524312
  3.0 35.2 %shard_map.46 = (bf16[3,512,512]{2,1,0:T(8,128)(2,1)S(1)}, bf16[512,512]{1,0:T(8,128)(2,1)S(1)}) custom-call(bf16[2,3,216,256]{3,2,1,0:T(8,128)(2,1)S(1)} %bitcast.6, f32[216,54]{1,0:T(8,128)S(1)} %bitcast.8, bf16[2,128,1024]{2,1,0:T(8,128)(2,1)S(1)} %bitcast.7), custom_call_target="tpu_custom_call" | custom-call | tf_op jit(solution)/shard_map/pallas_call | solution.py:481
  38.2 0.0 copy-start.2
  38.2 0.6 %copy-done.2 = s32[3]{0:T(128)S(1)} copy-done((s32[3]{0:T(128)S(1)}, s32[3]{0:T(128)}, u32[]{:S(2)}) %copy-start.2) | copy-done | bytes 36
  38.9 4.0 %shard_map.47 = bf16[3,2,128,1024]{3,2,1,0:T(8,128)(2,1)} custom-call(s32[3]{0:T(128)S(1)} %copy-done.2, bf16[3,512,512]{2,1,0:T(8,128)(2,1)S(1)} %get-tuple-element.7.elem_ref, bf16[512,512]{1,0:T(8,128)(2,1)S(1)} %get-tuple-element.8.spread_ref), custom_call_target="tpu_custom_call" | custom-call | tf_op jit(solution)/shard_map/pallas_call | solution.py:447
Async XLA Ops:
  0.9 1.1 %copy-start = (bf16[1,2,256,3,216]{2,4,3,1,0:T(8,128)(2,1)S(1)}, bf16[1,2,256,3,216]{2,4,3,1,0:T(8,128)(2,1)}, u32[]{:S(2)}) copy-start(bf16[1,2,256,3,216]{2,4,3,1,0:T(8,128)(2,1)} %param.4) | copy-start | bytes 1990660
  2.0 1.0 %copy-start.1 = (bf16[1,2,128,1024]{3,2,1,0:T(8,128)(2,1)S(1)}, bf16[1,2,128,1024]{3,2,1,0:T(8,128)(2,1)}, u32[]{:S(2)}) copy-start(bf16[1,2,128,1024]{3,2,1,0:T(8,128)(2,1)} %param.7) | copy-start | bytes 1572868
  38.2 0.7 %copy-start.2 = (s32[3]{0:T(128)S(1)}, s32[3]{0:T(128)}, u32[]{:S(2)}) copy-start(s32[3]{0:T(128)} %dirs_ref.1) | copy-start | bytes 40
